TPU v7x, 768 devices: a whole 4x8x12 slice. The times are simulated.
768 devices in a mesh: blk: 12 (over z_hi, x), group: 64 (over y, z_lo, core).
Axes of the slice: x: 4, y: 8, z: 12 (z_hi: 3, z_lo: 4; z = z_hi * 4 + z_lo), core: 2. Of those that a mesh axis runs over, the one named last changes fastest.
Arguments:
- picture_embeds_raw: bfloat16 [196608, 1152], P(('blk', 'group')), may hold values from -0.1796875 to 0.1796875
- caption_embeds_raw: bfloat16 [196608, 1152], P(('blk', 'group')), may hold values from -0.1796875 to 0.1796875
- sharpness_factor: float32 [], replicated, may hold values from 4 to 16
- additive_shift_term: float32 [], replicated, may hold values from -4 to -1
Outputs:
- row_loss: float32 [196608], P(('blk', 'group'))
- image_grad: bfloat16 [196608, 1152], P(('blk', 'group'))
- text_grad: bfloat16 [196608, 1152], P(('blk', 'group'))
All inputs are finite; a program needn't handle non-finite values.
Results may differ from a plain program's by a relative error of at most 0.009.
Values may be sent and summed in bfloat16 or wider, within the bound.
A program may use at most 64 MiB of HBM per device.

v0:
```python
import jax
import jax.numpy as jnp
from jax import lax
from jax.sharding import PartitionSpec as P


def passed_along(shard, axis, by):
    peers = lax.axis_size(axis)
    return lax.ppermute(shard, axis, [(i, (i + by) % peers) for i in range(peers)])


def normalize(raw):
    rawf = raw.astype(jnp.float32)
    norms = jnp.sqrt(jnp.sum(rawf * rawf, axis=-1, keepdims=True) + 1e-06)
    return ((rawf / norms).astype(jnp.bfloat16), norms)


def unnormalize(grads, raw, norms):
    rawf = raw.astype(jnp.float32)
    inner = jnp.sum(rawf * grads, axis=-1, keepdims=True)
    return ((grads - rawf * inner / (norms * norms)) / norms).astype(jnp.bfloat16)


def similarity_table(
    normalized_picture_entries,
    caption_group_slice,
    sharpness_factor,
    additive_shift_term,
    desired_polarity,
):
    couple_similarity = (
        jnp.dot(
            normalized_picture_entries, caption_group_slice.T, preferred_element_type=jnp.float32
        )
        * sharpness_factor
        + additive_shift_term
    )
    losses = jnp.sum(jax.nn.softplus(-desired_polarity * couple_similarity), axis=-1)
    couple_weight_factor = (
        -desired_polarity * jax.nn.sigmoid(-desired_polarity * couple_similarity) * sharpness_factor
    ).astype(jnp.bfloat16)
    image_part = jnp.dot(
        couple_weight_factor, caption_group_slice, preferred_element_type=jnp.float32
    )
    text_part = lax.dot_general(
        couple_weight_factor,
        normalized_picture_entries,
        (((0,), (0,)), ((), ())),
        preferred_element_type=jnp.float32,
    )
    return (losses, image_part, text_part)


def on_device(picture_embeds_raw, caption_embeds_raw, sharpness_factor, additive_shift_term):
    normalized_picture_entries, image_norms = normalize(picture_embeds_raw)
    text_unit, text_norms = normalize(caption_embeds_raw)
    rows = normalized_picture_entries.shape[0]
    width = normalized_picture_entries.shape[1]
    cycle_len = lax.axis_size("blk")
    window = min(5, cycle_len)
    own_labels = jnp.where(jnp.eye(rows, dtype=bool), 1.0, -1.0).astype(jnp.float32)
    mismatched_polarity = jnp.float32(-1.0)
    row_loss = jnp.zeros((rows,), jnp.float32)
    image_sum = jnp.zeros((rows, width), jnp.float32)
    current_tile_index = text_unit
    carried = jnp.zeros((rows, width), jnp.float32)
    for offset in range(window):
        if offset > 0:
            current_tile_index, carried = (
                passed_along(current_tile_index.astype(jnp.float32), "blk", 1).astype(
                    current_tile_index.dtype
                ),
                passed_along(carried, "blk", 1),
            )
        desired_polarity = own_labels if offset == 0 else mismatched_polarity
        losses, image_part, text_part = similarity_table(
            normalized_picture_entries,
            current_tile_index,
            sharpness_factor,
            additive_shift_term,
            desired_polarity,
        )
        row_loss = row_loss + losses
        image_sum = image_sum + image_part
        carried = carried + text_part
    text_sum = passed_along(carried, "blk", -(window - 1))
    rotated_captions = passed_along(text_unit, "group", 1)
    losses, image_part, text_part = similarity_table(
        normalized_picture_entries,
        rotated_captions,
        sharpness_factor,
        additive_shift_term,
        mismatched_polarity,
    )
    returned = passed_along(text_part.astype(jnp.bfloat16), "group", -1).astype(text_part.dtype)
    row_loss, image_sum, text_sum = (row_loss + losses, image_sum + image_part, text_sum + returned)
    image_grad = unnormalize(image_sum, picture_embeds_raw, image_norms)
    text_grad = unnormalize(text_sum, caption_embeds_raw, text_norms)
    return (row_loss, image_grad, text_grad)


def solution(mesh):
    in_specs = (P(("blk", "group"), None), P(("blk", "group"), None), P(), P())
    out_specs = (P(("blk", "group")), P(("blk", "group"), None), P(("blk", "group"), None))
    return jax.shard_map(
        on_device, mesh=mesh, in_specs=in_specs, out_specs=out_specs, check_vma=False
    )
```

profile of v0, /device:TPU:1, one launch (start us, length us, event | category | flops | bytes accessed | tf_op | source)
XLA Modules:
  0.0 706.8 jit_solution(3838496587810715874)
XLA Ops:
  1.3 1.3 fusion.3
  2.6 1.3 fusion.4
  5.9 3.9 collective-permute-start.5
  9.9 3.1 collective-permute-start
  13.0 47.4 %collective-permute-done = bf16[256,1152]{1,0:T(8,128)(2,1)S(1)} collective-permute-done((bf16[256,1152]{1,0:T(8,128)(2,1)S(1)}, bf16[256,1152]{1,0:T(8,128)(2,1)S(1)}, u32[]{:S(2)}, u32[]{:S(2)}) %collective-permute-start) | collective-permute-done | bytes 589856 | tf_op jit(solution)/shard_map/ppermute | solution.py:9
  61.3 1.9 collective-permute-start.6
  63.2 1.9 collective-permute-start.1
  65.1 44.7 %collective-permute-start.4 = (bf16[256,1152]{1,0:T(8,128)(2,1)S(1)}, bf16[256,1152]{1,0:T(8,128)(2,1)S(1)}, u32[]{:S(2)}, u32[]{:S(2)}) collective-permute-start(bf16[256,1152]{1,0:T(8,128)(2,1)S(1)} %fusion.10), channel_id=1, source_target_pairs={{0,1},{1,2},{2,3},{3,4},{4,5},{5,6},{6,7},{7,8},{8,9},{9,10},{10,1... | collective-permute-start | bytes 1769480 | tf_op jit(solution)/shard_map/ppermute | solution.py:9
  110.3 225.0 %collective-permute-done.1 = bf16[256,1152]{1,0:T(8,128)(2,1)S(1)} collective-permute-done((bf16[256,1152]{1,0:T(8,128)(2,1)S(1)}, bf16[256,1152]{1,0:T(8,128)(2,1)S(1)}, u32[]{:S(2)}, u32[]{:S(2)}) %collective-permute-start.1) | collective-permute-done | bytes 589856 | tf_op jit(solution)/shard_map/ppermute | solution.py:9
  335.2 1.9 collective-permute-start.2
  338.2 1.9 collective-permute-start.7
  341.0 2.5 collective-permute-start.10
  343.9 200.3 %collective-permute-done.2 = bf16[256,1152]{1,0:T(8,128)(2,1)S(1)} collective-permute-done((bf16[256,1152]{1,0:T(8,128)(2,1)S(1)}, bf16[256,1152]{1,0:T(8,128)(2,1)S(1)}, u32[]{:S(2)}, u32[]{:S(2)}) %collective-permute-start.2) | collective-permute-done | bytes 589856 | tf_op jit(solution)/shard_map/ppermute | solution.py:9
  544.2 1.9 collective-permute-start.3
  547.0 22.4 %collective-permute-done.7 = f32[256,1152]{1,0:T(8,128)S(1)} collective-permute-done((f32[256,1152]{1,0:T(8,128)S(1)}, f32[256,1152]{1,0:T(8,128)S(1)}, u32[]{:S(2)}, u32[]{:S(2)}) %collective-permute-start.7) | collective-permute-done | bytes 1179680 | tf_op jit(solution)/shard_map/ppermute | solution.py:9
  569.5 1.9 collective-permute-start.8
  572.3 10.1 %collective-permute-done.3 = bf16[256,1152]{1,0:T(8,128)(2,1)S(1)} collective-permute-done((bf16[256,1152]{1,0:T(8,128)(2,1)S(1)}, bf16[256,1152]{1,0:T(8,128)(2,1)S(1)}, u32[]{:S(2)}, u32[]{:S(2)}) %collective-permute-start.3) | collective-permute-done | bytes 589856 | tf_op jit(solution)/shard_map/ppermute | solution.py:9
  583.7 24.1 %collective-permute-done.8 = f32[256,1152]{1,0:T(8,128)S(1)} collective-permute-done((f32[256,1152]{1,0:T(8,128)S(1)}, f32[256,1152]{1,0:T(8,128)S(1)}, u32[]{:S(2)}, u32[]{:S(2)}) %collective-permute-start.8) | collective-permute-done | bytes 1179680 | tf_op jit(solution)/shard_map/ppermute | solution.py:9
  608.0 46.9 %collective-permute-start.9 = (f32[256,1152]{1,0:T(8,128)S(1)}, f32[256,1152]{1,0:T(8,128)S(1)}, u32[]{:S(2)}, u32[]{:S(2)}) collective-permute-start(f32[256,1152]{1,0:T(8,128)S(1)} %add.164), channel_id=1, source_target_pairs={{0,512},{64,576},{128,640},{192,704},{256,0},{320,64},{384,128},{4... | collective-permute-start | bytes 3538952 | tf_op jit(solution)/shard_map/ppermute | solution.py:9
  654.9 0.6 add_add_fusion
  655.5 0.7 fusion.5
  656.2 1.1 fusion.16
  657.3 48.0 %collective-permute-done.9 = f32[256,1152]{1,0:T(8,128)S(1)} collective-permute-done((f32[256,1152]{1,0:T(8,128)S(1)}, f32[256,1152]{1,0:T(8,128)S(1)}, u32[]{:S(2)}, u32[]{:S(2)}) %collective-permute-start.9) | collective-permute-done | bytes 1179680 | tf_op jit(solution)/shard_map/ppermute | solution.py:9
  705.6 1.2 fusion.15
  (33 shorter events, 8.4 us)
Async XLA Ops:
  0.6 3.3 copy-start.1
  5.9 55.0 %collective-permute-start.5 = (f32[256,1152]{1,0:T(8,128)S(1)}, f32[256,1152]{1,0:T(8,128)S(1)}, u32[]{:S(2)}, u32[]{:S(2)}) collective-permute-start(f32[256,1152]{1,0:T(8,128)S(1)} %fusion.46), channel_id=1, source_target_pairs={{0,64},{64,128},{128,192},{192,256},{256,320},{320,384},{384,448},... | collective-permute-start | bytes 3538952 | tf_op jit(solution)/shard_map/ppermute | solution.py:9
  9.9 50.5 %collective-permute-start = (bf16[256,1152]{1,0:T(8,128)(2,1)S(1)}, bf16[256,1152]{1,0:T(8,128)(2,1)S(1)}, u32[]{:S(2)}, u32[]{:S(2)}) collective-permute-start(bf16[256,1152]{1,0:T(8,128)(2,1)S(1)} %fusion.10), channel_id=1, source_target_pairs={{0,64},{64,128},{128,192},{192,256},{256,320},{320,384},{384,448},... | collective-permute-start | bytes 1769480 | tf_op jit(solution)/shard_map/ppermute | solution.py:9
  61.3 276.8 %collective-permute-start.6 = (f32[256,1152]{1,0:T(8,128)S(1)}, f32[256,1152]{1,0:T(8,128)S(1)}, u32[]{:S(2)}, u32[]{:S(2)}) collective-permute-start(f32[256,1152]{1,0:T(8,128)S(1)} %convolution_add_fusion), channel_id=1, source_target_pairs={{0,64},{64,128},{128,192},{192,256},{256,320},{320,384},{384,448},... | collective-permute-start | bytes 3538952 | tf_op jit(solution)/shard_map/ppermute | solution.py:9
  63.2 272.0 %collective-permute-start.1 = (bf16[256,1152]{1,0:T(8,128)(2,1)S(1)}, bf16[256,1152]{1,0:T(8,128)(2,1)S(1)}, u32[]{:S(2)}, u32[]{:S(2)}) collective-permute-start(bf16[256,1152]{1,0:T(8,128)(2,1)S(1)} %collective-permute-done), channel_id=1, source_target_pairs={{0,64},{64,128},{128,192},{192,256},{256,320},{320,384},{384,448},... | collective-permute-start | bytes 1769480 | tf_op jit(solution)/shard_map/ppermute | solution.py:9
  65.1 275.0 %collective-permute-start.4 = (bf16[256,1152]{1,0:T(8,128)(2,1)S(1)}, bf16[256,1152]{1,0:T(8,128)(2,1)S(1)}, u32[]{:S(2)}, u32[]{:S(2)}) collective-permute-start(bf16[256,1152]{1,0:T(8,128)(2,1)S(1)} %fusion.10), channel_id=1, source_target_pairs={{0,1},{1,2},{2,3},{3,4},{4,5},{5,6},{6,7},{7,8},{8,9},{9,10},{10,1... | collective-permute-start | bytes 1769480 | tf_op jit(solution)/shard_map/ppermute | solution.py:9
  335.2 209.0 %collective-permute-start.2 = (bf16[256,1152]{1,0:T(8,128)(2,1)S(1)}, bf16[256,1152]{1,0:T(8,128)(2,1)S(1)}, u32[]{:S(2)}, u32[]{:S(2)}) collective-permute-start(bf16[256,1152]{1,0:T(8,128)(2,1)S(1)} %collective-permute-done.1), channel_id=1, source_target_pairs={{0,64},{64,128},{128,192},{192,256},{256,320},{320,384},{384,448},... | collective-permute-start | bytes 1769480 | tf_op jit(solution)/shard_map/ppermute | solution.py:9
  338.2 231.2 %collective-permute-start.7 = (f32[256,1152]{1,0:T(8,128)S(1)}, f32[256,1152]{1,0:T(8,128)S(1)}, u32[]{:S(2)}, u32[]{:S(2)}) collective-permute-start(f32[256,1152]{1,0:T(8,128)S(1)} %add.162), channel_id=1, source_target_pairs={{0,64},{64,128},{128,192},{192,256},{256,320},{320,384},{384,448},... | collective-permute-start | bytes 3538952 | tf_op jit(solution)/shard_map/ppermute | solution.py:9
  341.0 316.3 %collective-permute-start.10 = (bf16[256,1152]{1,0:T(8,128)(2,1)S(1)}, bf16[256,1152]{1,0:T(8,128)(2,1)S(1)}, u32[]{:S(2)}, u32[]{:S(2)}) collective-permute-start(bf16[256,1152]{1,0:T(8,128)(2,1)S(1)} %convolution_convert_fusion), channel_id=1, source_target_pairs={{0,63},{1,0},{2,1},{3,2},{4,3},{5,4},{6,5},{7,6},{8,7},{9,8},{10,9... | collective-permute-start | bytes 1769480 | tf_op jit(solution)/shard_map/ppermute | solution.py:9
  544.2 38.2 %collective-permute-start.3 = (bf16[256,1152]{1,0:T(8,128)(2,1)S(1)}, bf16[256,1152]{1,0:T(8,128)(2,1)S(1)}, u32[]{:S(2)}, u32[]{:S(2)}) collective-permute-start(bf16[256,1152]{1,0:T(8,128)(2,1)S(1)} %collective-permute-done.2), channel_id=1, source_target_pairs={{0,64},{64,128},{128,192},{192,256},{256,320},{320,384},{384,448},... | collective-permute-start | bytes 1769480 | tf_op jit(solution)/shard_map/ppermute | solution.py:9
  569.5 38.3 %collective-permute-start.8 = (f32[256,1152]{1,0:T(8,128)S(1)}, f32[256,1152]{1,0:T(8,128)S(1)}, u32[]{:S(2)}, u32[]{:S(2)}) collective-permute-start(f32[256,1152]{1,0:T(8,128)S(1)} %add.163), channel_id=1, source_target_pairs={{0,64},{64,128},{128,192},{192,256},{256,320},{320,384},{384,448},... | collective-permute-start | bytes 3538952 | tf_op jit(solution)/shard_map/ppermute | solution.py:9
  583.7 71.8 %copy-start = (bf16[256,1152]{1,0:T(8,128)(2,1)S(1)}, bf16[256,1152]{1,0:T(8,128)(2,1)}, u32[]{:S(2)}) copy-start(bf16[256,1152]{1,0:T(8,128)(2,1)} %param.4) | copy-start | bytes 1769476
  608.0 97.3 %collective-permute-start.9 = (f32[256,1152]{1,0:T(8,128)S(1)}, f32[256,1152]{1,0:T(8,128)S(1)}, u32[]{:S(2)}, u32[]{:S(2)}) collective-permute-start(f32[256,1152]{1,0:T(8,128)S(1)} %add.164), channel_id=1, source_target_pairs={{0,512},{64,576},{128,640},{192,704},{256,0},{320,64},{384,128},{4... | collective-permute-start | bytes 3538952 | tf_op jit(solution)/shard_map/ppermute | solution.py:9
where the time goes:
time: 707 us
  waiting for transfers between devices  577 us (82%)
  starting transfers between devices  113 us (16%)
  matrix products  7.97 us (1%)
    ppermute x11, waiting for transfers between devices, passed_along(): lax.ppermute(shard, axis, [(i, (i + by) % peers) for i in range(peers)])  577 us
    ppermute x11, starting transfers between devices, passed_along(): lax.ppermute(shard, axis, [(i, (i + by) % peers) for i in range(peers)])  113 us
  transfers between devices with their start and end apart: 11, of which 7 were waited for; matrix products, arithmetic and copies ran while one was open for 1% of the time, Pallas kernels for 0%

commit v1 on v0

v1 whole, which is shorter than its diff:
```python
import functools
import jax
import jax.numpy as jnp
from jax import lax
from jax.experimental import pallas as pl
from jax.experimental.pallas import tpu as pltpu
from jax.sharding import PartitionSpec as P

MESH = pl.DeviceIdType.MESH
NX = 4
CHUNKS = 8
IMAGE, TEXT = 0, 1


def partners():
    blk, group = lax.axis_index("blk"), lax.axis_index("group")
    n_blk, n_group = lax.axis_size("blk"), lax.axis_size("group")
    x = lax.rem(blk, NX)
    plane = blk - x
    return dict(
        x=x,
        ahead=(lax.rem(blk + NX, n_blk), group),
        behind=(lax.rem(blk + n_blk - NX, n_blk), group),
        along=[None] + [(plane + lax.rem(x + d, NX), group) for d in range(1, NX)],
        after=(blk, lax.rem(group + 1, n_group)),
        before=(blk, lax.rem(group + n_group - 1, n_group)),
    )


def kernel(
    scal, pic, cap, loss_out, image_out, text_out,
    raw, unit, inv, block, near, acc, loss_acc,
    in_sem, out_sem, z_send, z_recv, x_send, x_recv, g_send, g_recv,
):
    rows, width = unit.shape[1], unit.shape[2]
    part = rows // CHUNKS
    sharp, shift = scal[0], scal[1]
    who = partners()
    x = who["x"]

    loads = [
        pltpu.make_async_copy(src, raw.at[side], in_sem.at[side])
        for side, src in ((IMAGE, pic), (TEXT, cap))
    ]
    for load in loads:
        load.start()

    barrier = pltpu.get_barrier_semaphore()
    others = [who["ahead"], who["behind"], who["after"], who["before"]] + who["along"][1:]
    for other in others:
        pl.semaphore_signal(barrier, inc=1, device_id=other, device_id_type=MESH)

    def z_copy(side, k):
        return pltpu.make_async_remote_copy(
            src_ref=unit.at[side, pl.ds(k * part, part)],
            dst_ref=block.at[side, k, 0],
            send_sem=z_send.at[side, k],
            recv_sem=z_recv.at[side, k],
            device_id=who["ahead"] if side == TEXT else who["behind"],
            device_id_type=MESH,
        )

    def x_copy(side, d, k, late):
        own = unit.at[side, pl.ds(k * part, part)]
        return pltpu.make_async_remote_copy(
            src_ref=block.at[side, k, 0] if late else own,
            dst_ref=block.at[side, k, d],
            send_sem=x_send.at[side, d - 1, k],
            recv_sem=x_recv.at[side, d - 1, k],
            device_id=who["along"][d],
            device_id_type=MESH,
        )

    def g_copy(side, k):
        return pltpu.make_async_remote_copy(
            src_ref=unit.at[side, pl.ds(k * part, part)],
            dst_ref=near.at[side, pl.ds(k * part, part)],
            send_sem=g_send.at[side, k],
            recv_sem=g_recv.at[side, k],
            device_id=who["after"] if side == TEXT else who["before"],
            device_id_type=MESH,
        )

    for side in (IMAGE, TEXT):
        loads[side].wait()

        @pl.loop(0, CHUNKS)
        def _(k):
            at = pl.ds(k * part, part)
            rawf = raw[side, at].astype(jnp.float32)
            scale = 1.0 / jnp.sqrt(jnp.sum(rawf * rawf, axis=-1, keepdims=True) + 1e-06)
            inv[side, at] = scale
            unit[side, at] = (rawf * scale).astype(jnp.bfloat16)

    pl.semaphore_wait(barrier, len(others))

    @pl.loop(0, CHUNKS)
    def _(k):
        for side in (IMAGE, TEXT):
            z_copy(side, k).start()

    @pl.loop(0, CHUNKS)
    def _(k):
        for d in range(1, NX):

            @pl.when(x + d < NX)
            def _():
                x_copy(TEXT, d, k, False).start()

            @pl.when(x + d >= NX)
            def _():
                x_copy(IMAGE, d, k, False).start()

    def logits(mine, theirs):
        dots = lax.dot_general(
            mine, theirs, (((1,), (1,)), ((), ())), preferred_element_type=jnp.float32
        )
        return dots * sharp + shift

    def soft(v):
        small = jnp.exp(-jnp.abs(v))
        plus = jnp.maximum(v, 0.0) + jnp.log1p(small)
        return plus, jnp.where(v >= 0.0, 1.0, small) / (1.0 + small)

    lanes = loss_acc.shape[1]
    same = lax.broadcasted_iota(jnp.int32, (rows, rows), 0) == lax.broadcasted_iota(
        jnp.int32, (rows, rows), 1
    )
    label = jnp.where(same, 1.0, -1.0)
    plus, sig = soft(-label * logits(unit[IMAGE], unit[TEXT]))
    loss_acc[...] = sum(plus[:, i : i + lanes] for i in range(0, rows, lanes))
    coef = (-label * sig * sharp).astype(jnp.bfloat16)
    acc[IMAGE] = jnp.dot(coef, unit[TEXT], preferred_element_type=jnp.float32)
    acc[TEXT] = lax.dot_general(
        coef, unit[IMAGE], (((0,), (0,)), ((), ())), preferred_element_type=jnp.float32
    )

    def score_texts(theirs):
        plus, sig = soft(logits(unit[IMAGE], theirs))
        loss_acc[...] += plus
        coef = (sig * sharp).astype(jnp.bfloat16)
        acc[IMAGE] += jnp.dot(coef, theirs, preferred_element_type=jnp.float32)

    def score_images(theirs):
        sig = 1.0 / (1.0 + jnp.exp(-logits(unit[TEXT], theirs)))
        coef = (sig * sharp).astype(jnp.bfloat16)
        acc[TEXT] += jnp.dot(coef, theirs, preferred_element_type=jnp.float32)

    def finish_round(k):
        for side, score in ((TEXT, score_texts), (IMAGE, score_images)):
            for d in range(1, NX):
                x_copy(side, d, k, False).wait_recv()
            score(block[side, k].reshape(NX * part, width))

    @pl.loop(0, CHUNKS)
    def _(k):
        for side in (IMAGE, TEXT):
            z_copy(side, k).wait_recv()
        for d in range(1, NX):

            @pl.when(x + d >= NX)
            def _():
                x_copy(TEXT, d, k, True).start()

            @pl.when(x + d < NX)
            def _():
                x_copy(IMAGE, d, k, True).start()

        for side in (IMAGE, TEXT):
            g_copy(side, k).start()

        @pl.when(k > 0)
        def _():
            finish_round(k - 1)

    finish_round(CHUNKS - 1)

    per = NX * part
    for side, score in ((TEXT, score_texts), (IMAGE, score_images)):
        for p in range(rows // per):
            for k in range(p * NX, (p + 1) * NX):
                g_copy(side, k).wait_recv()
            score(near[side, p * per : (p + 1) * per])

    loss_out[...] = jnp.sum(loss_acc[...].T, axis=0, keepdims=True)

    def out_copy(side, k):
        at = pl.ds(k * part, part)
        out = image_out if side == IMAGE else text_out
        return pltpu.make_async_copy(raw.at[side, at], out.at[at], out_sem.at[side, k])

    for side in (IMAGE, TEXT):

        @pl.loop(0, CHUNKS)
        def _(k):
            at = pl.ds(k * part, part)
            rawf = raw[side, at].astype(jnp.float32)
            grads = acc[side, at]
            scale = inv[side, at]
            inner = jnp.sum(rawf * grads, axis=-1, keepdims=True)
            raw[side, at] = ((grads - rawf * (inner * scale * scale)) * scale).astype(jnp.bfloat16)
            out_copy(side, k).start()

    @pl.loop(0, CHUNKS)
    def _(k):
        for side in (IMAGE, TEXT):
            z_copy(side, k).wait_send()
            g_copy(side, k).wait_send()
            for d in range(1, NX):
                x_copy(side, d, k, False).wait_send()
            out_copy(side, k).wait()


def on_device(picture_embeds_raw, caption_embeds_raw, sharpness_factor, additive_shift_term):
    rows, width = picture_embeds_raw.shape
    part = rows // CHUNKS
    kind = picture_embeds_raw.dtype
    vmem, any_ = pl.BlockSpec(memory_space=pltpu.VMEM), pl.BlockSpec(memory_space=pl.ANY)
    dma = pltpu.SemaphoreType.DMA
    scalars = jnp.stack([sharpness_factor, additive_shift_term]).astype(jnp.float32)
    loss, image_grad, text_grad = pl.pallas_call(
        kernel,
        out_shape=(
            jax.ShapeDtypeStruct((1, rows), jnp.float32),
            jax.ShapeDtypeStruct((rows, width), kind),
            jax.ShapeDtypeStruct((rows, width), kind),
        ),
        in_specs=[pl.BlockSpec(memory_space=pltpu.SMEM), any_, any_],
        out_specs=(vmem, any_, any_),
        scratch_shapes=[
            pltpu.VMEM((2, rows, width), kind),
            pltpu.VMEM((2, rows, width), jnp.bfloat16),
            pltpu.VMEM((2, rows, 1), jnp.float32),
            pltpu.VMEM((2, CHUNKS, NX, part, width), jnp.bfloat16),
            pltpu.VMEM((2, rows, width), jnp.bfloat16),
            pltpu.VMEM((2, rows, width), jnp.float32),
            pltpu.VMEM((rows, NX * part), jnp.float32),
            dma((2,)),
            dma((2, CHUNKS)),
            dma((2, CHUNKS)),
            dma((2, CHUNKS)),
            dma((2, NX - 1, CHUNKS)),
            dma((2, NX - 1, CHUNKS)),
            dma((2, CHUNKS)),
            dma((2, CHUNKS)),
        ],
        compiler_params=pltpu.CompilerParams(
            collective_id=0, has_side_effects=True, vmem_limit_bytes=40 << 20
        ),
        name="paired_blocks",
    )(scalars, picture_embeds_raw, caption_embeds_raw)
    return loss.reshape(rows), image_grad, text_grad


def solution(mesh):
    in_specs = (P(("blk", "group"), None), P(("blk", "group"), None), P(), P())
    out_specs = (P(("blk", "group")), P(("blk", "group"), None), P(("blk", "group"), None))
    return jax.shard_map(
        on_device, mesh=mesh, in_specs=in_specs, out_specs=out_specs, check_vma=False
    )
```

time: 707 us -> 99.6 us (0.14)
  the two profiles are of different devices: /device:TPU:1 before, /device:TPU:216 now
where the time goes in v1:
time: 99.6 us; the launch traced here: 99.4 us
  Pallas kernels  93 us (93%)
  local copies, waits for them, and re-layouts  4.32 us (4%)
  between operations  1.93 us (2%)
    pallas_call x1, Pallas kernels, on_device(): pl.pallas_call(kernel, out_shape=(jax.ShapeDtypeStruct((1, rows), jnp.flo...  93 us
    unnamed x7, local copies, waits for them, and re-layouts  4.32 us

profile of v1, /device:TPU:216, one launch (start us, length us, event | category | flops | bytes accessed | tf_op | source)
XLA Modules:
  0.0 99.4 jit_solution(17866007057757896009)
XLA Ops:
  1.9 0.1 pad_maximum_fusion.scal
  2.0 0.0 copy-start
  2.0 1.1 %copy-done = bf16[256,1152]{1,0:T(8,128)(2,1)S(1)} copy-done((bf16[256,1152]{1,0:T(8,128)(2,1)S(1)}, bf16[256,1152]{1,0:T(8,128)(2,1)}, u32[]{:S(2)}) %copy-start) | copy-done | bytes 589848
  3.1 0.0 copy-start.1
  3.1 1.1 %copy-done.1 = bf16[256,1152]{1,0:T(8,128)(2,1)S(1)} copy-done((bf16[256,1152]{1,0:T(8,128)(2,1)S(1)}, bf16[256,1152]{1,0:T(8,128)(2,1)}, u32[]{:S(2)}) %copy-start.1) | copy-done | bytes 589848
  4.1 93.0 %paired_blocks.1 = (f32[1,256]{1,0:T(1,128)S(1)}, bf16[256,1152]{1,0:T(8,128)(2,1)S(1)}, bf16[256,1152]{1,0:T(8,128)(2,1)S(1)}) custom-call(f32[2]{0:T(128)S(1)} %pad_maximum_fusion.scal, bf16[256,1152]{1,0:T(8,128)(2,1)S(1)} %copy-done, bf16[256,1152]{1,0:T(8,128)(2,1)S(1)} %copy-done.1), custom_call_target="tpu_custom_call" | custom-call | tf_op jit(solution)/shard_map/paired_blocks/pallas_call | solution.py:221
  97.2 0.6 copy.12
  97.7 0.8 copy.13
  98.5 0.8 copy.14
Async XLA Ops:
  2.0 1.1 %copy-start = (bf16[256,1152]{1,0:T(8,128)(2,1)S(1)}, bf16[256,1152]{1,0:T(8,128)(2,1)}, u32[]{:S(2)}) copy-start(bf16[256,1152]{1,0:T(8,128)(2,1)} %pic.1) | copy-start | bytes 1769476
  3.1 1.1 %copy-start.1 = (bf16[256,1152]{1,0:T(8,128)(2,1)S(1)}, bf16[256,1152]{1,0:T(8,128)(2,1)}, u32[]{:S(2)}) copy-start(bf16[256,1152]{1,0:T(8,128)(2,1)} %cap.1) | copy-start | bytes 1769476

commit v2 on v1

v2 whole, which is shorter than its diff:
```python
import functools
import jax
import jax.numpy as jnp
from jax import lax
from jax.experimental import pallas as pl
from jax.experimental.pallas import tpu as pltpu
from jax.sharding import PartitionSpec as P

MESH = pl.DeviceIdType.MESH
NX = 4
CHUNKS = 8
WINDOW = 3
G_LAG = 0
IMAGE, TEXT = 0, 1


def partners():
    blk, group = lax.axis_index("blk"), lax.axis_index("group")
    n_blk, n_group = lax.axis_size("blk"), lax.axis_size("group")
    x = lax.rem(blk, NX)
    plane = blk - x
    return dict(
        x=x,
        ahead=(lax.rem(blk + NX, n_blk), group),
        behind=(lax.rem(blk + n_blk - NX, n_blk), group),
        along=[None] + [(plane + lax.rem(x + d, NX), group) for d in range(1, NX)],
        after=(blk, lax.rem(group + 1, n_group)),
        before=(blk, lax.rem(group + n_group - 1, n_group)),
    )


def exchange(
    scal, pic, cap,
    image_acc, text_acc, image_raw, text_raw, loss_out,
    unit, block, loss_acc,
    in_sem, z_send, z_recv, x_send, x_recv, g_send, g_recv,
):
    rows, width = unit.shape[1], unit.shape[2]
    part = rows // CHUNKS
    half = rows // 2
    per = NX * part
    g_at = CHUNKS * per
    sharp, shift = scal[0], scal[1]
    who = partners()
    x = who["x"]

    loads = [
        pltpu.make_async_copy(src, dst, in_sem.at[side])
        for side, src, dst in ((IMAGE, pic, image_raw), (TEXT, cap, text_raw))
    ]
    for load in loads:
        load.start()

    barrier = pltpu.get_barrier_semaphore()
    others = [who["ahead"], who["behind"], who["after"], who["before"]] + who["along"][1:]
    for other in others:
        pl.semaphore_signal(barrier, inc=1, device_id=other, device_id_type=MESH)

    def z_copy(side, k):
        return pltpu.make_async_remote_copy(
            src_ref=unit.at[side, pl.ds(k * part, part)],
            dst_ref=block.at[side, pl.ds(k * per, part)],
            send_sem=z_send.at[side, k],
            recv_sem=z_recv.at[side, k],
            device_id=who["ahead"] if side == TEXT else who["behind"],
            device_id_type=MESH,
        )

    def x_copy(side, d, k, late):
        own = unit.at[side, pl.ds(k * part, part)]
        return pltpu.make_async_remote_copy(
            src_ref=block.at[side, pl.ds(k * per, part)] if late else own,
            dst_ref=block.at[side, pl.ds(k * per + d * part, part)],
            send_sem=x_send.at[side, d - 1, k],
            recv_sem=x_recv.at[side, d - 1, k],
            device_id=who["along"][d],
            device_id_type=MESH,
        )

    def g_copy(side, k):
        to = lax.rem(k * part + half, rows)
        return pltpu.make_async_remote_copy(
            src_ref=unit.at[side, pl.ds(k * part, part)],
            dst_ref=block.at[side, pl.ds(g_at + to, part)],
            send_sem=g_send.at[side, k],
            recv_sem=g_recv.at[side, k],
            device_id=who["after"] if side == TEXT else who["before"],
            device_id_type=MESH,
        )

    for side, raw in ((IMAGE, image_raw), (TEXT, text_raw)):
        loads[side].wait()

        @pl.loop(0, 2)
        def _(k):
            at = pl.ds(k * half, half)
            rawf = raw[at].astype(jnp.float32)
            scale = 1.0 / jnp.sqrt(jnp.sum(rawf * rawf, axis=-1, keepdims=True) + 1e-06)
            unit[side, at] = (rawf * scale).astype(jnp.bfloat16)

    pl.semaphore_wait(barrier, len(others))

    for k in range(WINDOW):
        for side in (IMAGE, TEXT):
            z_copy(side, k).start()

    @pl.loop(0, CHUNKS)
    def _(k):
        for d in range(1, NX):

            @pl.when(x + d < NX)
            def _():
                x_copy(TEXT, d, k, False).start()

            @pl.when(x + d >= NX)
            def _():
                x_copy(IMAGE, d, k, False).start()

    def logits(mine, theirs):
        dots = lax.dot_general(
            mine, theirs, (((1,), (1,)), ((), ())), preferred_element_type=jnp.float32
        )
        return dots * sharp + shift

    def soft(v):
        small = jnp.exp(-jnp.abs(v))
        plus = jnp.maximum(v, 0.0) + jnp.log1p(small)
        return plus, jnp.where(v >= 0.0, 1.0, small) / (1.0 + small)

    lanes = loss_acc.shape[1]

    def narrowed(plus):
        return sum(plus[:, i : i + lanes] for i in range(0, plus.shape[1], lanes))

    same = lax.broadcasted_iota(jnp.int32, (rows, rows), 0) == lax.broadcasted_iota(
        jnp.int32, (rows, rows), 1
    )
    label = jnp.where(same, 1.0, -1.0)
    plus, sig = soft(-label * logits(unit[IMAGE], unit[TEXT]))
    loss_acc[...] = narrowed(plus)
    coef = (-label * sig * sharp).astype(jnp.bfloat16)
    image_acc[...] = jnp.dot(coef, unit[TEXT], preferred_element_type=jnp.float32)
    text_acc[...] = lax.dot_general(
        coef, unit[IMAGE], (((0,), (0,)), ((), ())), preferred_element_type=jnp.float32
    )

    def score(at):
        texts, images = block[TEXT, at], block[IMAGE, at]
        plus, sig = soft(logits(unit[IMAGE], texts))
        back = 1.0 / (1.0 + jnp.exp(-logits(unit[TEXT], images)))
        loss_acc[...] += narrowed(plus)
        image_acc[...] += jnp.dot(
            (sig * sharp).astype(jnp.bfloat16), texts, preferred_element_type=jnp.float32
        )
        text_acc[...] += jnp.dot(
            (back * sharp).astype(jnp.bfloat16), images, preferred_element_type=jnp.float32
        )

    def await_round(k):
        for side in (TEXT, IMAGE):
            for d in range(1, NX):
                x_copy(side, d, k, False).wait_recv()

    def start_near(k):
        for side in (IMAGE, TEXT):
            g_copy(side, k).start()

    @pl.loop(0, CHUNKS)
    def _(k):
        for side in (IMAGE, TEXT):
            z_copy(side, k).wait_recv()
        for d in range(1, NX):

            @pl.when(x + d >= NX)
            def _():
                x_copy(TEXT, d, k, True).start()

            @pl.when(x + d < NX)
            def _():
                x_copy(IMAGE, d, k, True).start()

        @pl.when(k + WINDOW < CHUNKS)
        def _():
            for side in (IMAGE, TEXT):
                z_copy(side, k + WINDOW).start()

        @pl.when(k >= G_LAG)
        def _():
            start_near(k - G_LAG)

        @pl.when(k > 0)
        def _():
            await_round(k - 1)
            score(pl.ds((k - 1) * per, per))

    for k in range(CHUNKS - G_LAG, CHUNKS):
        start_near(k)
    for k in range(CHUNKS // 2):
        for side in (TEXT, IMAGE):
            g_copy(side, k).wait_recv()
    score(slice(g_at + half, g_at + rows))
    await_round(CHUNKS - 1)
    for k in range(CHUNKS // 2, CHUNKS):
        for side in (TEXT, IMAGE):
            g_copy(side, k).wait_recv()
    score(slice(g_at - per, g_at + half))

    loss_out[...] = jnp.sum(loss_acc[...].T, axis=0, keepdims=True)

    @pl.loop(0, CHUNKS)
    def _(k):
        for side in (IMAGE, TEXT):
            z_copy(side, k).wait_send()
            g_copy(side, k).wait_send()
            for d in range(1, NX):
                x_copy(side, d, k, False).wait_send()


def finish(
    image_acc, text_acc, image_raw, text_raw, loss, loss_out, image_out, text_out, grad, out_sem
):
    rows = image_acc.shape[0]
    loss_out[...] = loss[0]
    pieces = out_sem.shape[1]
    part = rows // pieces
    copies = []
    for side, acc, raw, out in (
        (IMAGE, image_acc, image_raw, image_out),
        (TEXT, text_acc, text_raw, text_out),
    ):
        for p in range(pieces):
            at = pl.ds(p * part, part)
            rawf = raw[at].astype(jnp.float32)
            grads = acc[at]
            scale = 1.0 / jnp.sqrt(jnp.sum(rawf * rawf, axis=-1, keepdims=True) + 1e-06)
            inner = jnp.sum(rawf * grads, axis=-1, keepdims=True)
            grad[side, at] = ((grads - rawf * (inner * scale * scale)) * scale).astype(grad.dtype)
            copies.append(
                pltpu.make_async_copy(grad.at[side, at], out.at[at], out_sem.at[side, p])
            )
            copies[-1].start()
    for copy in copies:
        copy.wait()


def on_device(picture_embeds_raw, caption_embeds_raw, sharpness_factor, additive_shift_term):
    rows, width = picture_embeds_raw.shape
    part = rows // CHUNKS
    kind = picture_embeds_raw.dtype
    vmem, any_ = pl.BlockSpec(memory_space=pltpu.VMEM), pl.BlockSpec(memory_space=pl.ANY)
    hbm = pl.BlockSpec(memory_space=pltpu.HBM)
    dma = pltpu.SemaphoreType.DMA
    scalars = jnp.stack([sharpness_factor, additive_shift_term]).astype(jnp.float32)
    sums = pl.pallas_call(
        exchange,
        out_shape=(
            pltpu.VMEM((rows, width), jnp.float32),
            pltpu.VMEM((rows, width), jnp.float32),
            pltpu.VMEM((rows, width), kind),
            pltpu.VMEM((rows, width), kind),
            pltpu.VMEM((1, rows), jnp.float32),
        ),
        in_specs=[pl.BlockSpec(memory_space=pltpu.SMEM), hbm, hbm],
        out_specs=(vmem,) * 5,
        scratch_shapes=[
            pltpu.VMEM((2, rows, width), jnp.bfloat16),
            pltpu.VMEM((2, (NX + 1) * rows, width), jnp.bfloat16),
            pltpu.VMEM((rows, min(128, NX * part)), jnp.float32),
            dma((2,)),
            dma((2, CHUNKS)),
            dma((2, CHUNKS)),
            dma((2, NX - 1, CHUNKS)),
            dma((2, NX - 1, CHUNKS)),
            dma((2, CHUNKS)),
            dma((2, CHUNKS)),
        ],
        compiler_params=pltpu.CompilerParams(
            collective_id=0, has_side_effects=True, vmem_limit_bytes=28 << 20
        ),
        name="exchange",
    )(
        scalars,
        pltpu.with_memory_space_constraint(picture_embeds_raw, pltpu.HBM),
        pltpu.with_memory_space_constraint(caption_embeds_raw, pltpu.HBM),
    )
    return pl.pallas_call(
        finish,
        out_shape=(
            jax.ShapeDtypeStruct((rows,), jnp.float32),
            jax.ShapeDtypeStruct((rows, width), kind),
            jax.ShapeDtypeStruct((rows, width), kind),
        ),
        in_specs=[vmem] * 5,
        out_specs=(vmem, any_, any_),
        scratch_shapes=[pltpu.VMEM((2, rows, width), kind), dma((2, 2))],
        compiler_params=pltpu.CompilerParams(vmem_limit_bytes=16 << 20),
        name="finish",
    )(*sums)


def solution(mesh):
    in_specs = (P(("blk", "group"), None), P(("blk", "group"), None), P(), P())
    out_specs = (P(("blk", "group")), P(("blk", "group"), None), P(("blk", "group"), None))
    return jax.shard_map(
        on_device, mesh=mesh, in_specs=in_specs, out_specs=out_specs, check_vma=False
    )
```

time: 99.6 us -> 90.9 us (0.913)
  the two profiles are of different devices: /device:TPU:216 before, /device:TPU:8 now
where the time goes in v2:
time: 90.9 us; the launch traced here: 90.7 us
  Pallas kernels  88.7 us (98%)
  between operations  1.93 us (2%)
    pallas_call x1, Pallas kernels, on_device(): pl.pallas_call(exchange, out_shape=(pltpu.VMEM((rows, width), jnp.float32...  86.4 us
    pallas_call x1, Pallas kernels, on_device(): pl.pallas_call(finish, out_shape=(jax.ShapeDtypeStruct((rows,), jnp.float...  2.24 us

profile of v2, /device:TPU:8, one launch (start us, length us, event | category | flops | bytes accessed | tf_op | source)
XLA Modules:
  0.0 90.7 jit_solution(17185345088360766473)
XLA Ops:
  1.9 0.1 pad_maximum_fusion.scal
  2.0 86.4 %exchange.1 = (f32[256,1152]{1,0:T(8,128)S(1)}, f32[256,1152]{1,0:T(8,128)S(1)}, bf16[256,1152]{1,0:T(8,128)(2,1)S(1)}, bf16[256,1152]{1,0:T(8,128)(2,1)S(1)}, f32[1,256]{1,0:T(1,128)S(1)}) custom-call(f32[2]{0:T(128)S(1)} %pad_maximum_fusion.scal, bf16[256,1152]{1,0:T(8,128)(2,1)} %pic.1, bf16[256,1152]{1,0:T(8,128)(2,1)} %cap.1), custom_call_target="tpu_custom_call" | custom-call | tf_op jit(solution)/shard_map/exchange/pallas_call | solution.py:254
  88.4 2.2 %finish.1 = (f32[256]{0:T(256)}, bf16[256,1152]{1,0:T(8,128)(2,1)}, bf16[256,1152]{1,0:T(8,128)(2,1)}) custom-call(f32[256,1152]{1,0:T(8,128)S(1)} %get-tuple-element.8.image_acc, f32[256,1152]{1,0:T(8,128)S(1)} %get-tuple-element.9.text_acc, bf16[256,1152]{1,0:T(8,128)(2,1)S(1)} %get-tuple-element.10.image_raw, ...), custom_call_target="tpu_custom_call" | custom-call | tf_op jit(solution)/shard_map/finish/pallas_call | solution.py:286

commit v3 on v2

--- a/solution.py
+++ b/solution.py
@@ -9,8 +9,9 @@
 MESH = pl.DeviceIdType.MESH
 NX = 4
 CHUNKS = 8
-WINDOW = 3
-G_LAG = 0
+RUN = 4
+G_LEAD = 1
+X_ORDER = (2, 1, 3)
 IMAGE, TEXT = 0, 1
 
 
@@ -19,8 +20,16 @@
     n_blk, n_group = lax.axis_size("blk"), lax.axis_size("group")
     x = lax.rem(blk, NX)
     plane = blk - x
+    lane = lax.rem(group // 2, RUN)
+    core = lax.rem(group, 2)
+    wraps = (core == 1) & (lane == RUN - 1)
     return dict(
         x=x,
+        window=jnp.where(lane == 0, CHUNKS, jnp.where(wraps, 6, 4)),
+        lead={
+            TEXT: jnp.where(wraps, CHUNKS, G_LEAD),
+            IMAGE: G_LEAD,
+        },
         ahead=(lax.rem(blk + NX, n_blk), group),
         behind=(lax.rem(blk + n_blk - NX, n_blk), group),
         along=[None] + [(plane + lax.rem(x + d, NX), group) for d in range(1, NX)],
@@ -30,7 +39,7 @@
 
 
 def exchange(
-    scal, pic, cap,
+    sharp_ref, shift_ref, pic, cap,
     image_acc, text_acc, image_raw, text_raw, loss_out,
     unit, block, loss_acc,
     in_sem, z_send, z_recv, x_send, x_recv, g_send, g_recv,
@@ -40,16 +49,18 @@
     half = rows // 2
     per = NX * part
     g_at = CHUNKS * per
-    sharp, shift = scal[0], scal[1]
+    sharp, shift = sharp_ref[0, 0], shift_ref[0, 0]
     who = partners()
     x = who["x"]
 
-    loads = [
-        pltpu.make_async_copy(src, dst, in_sem.at[side])
-        for side, src, dst in ((IMAGE, pic, image_raw), (TEXT, cap, text_raw))
-    ]
-    for load in loads:
-        load.start()
+    def load(h, side, src, dst):
+        at = pl.ds(h * half, half)
+        return pltpu.make_async_copy(src.at[at], dst.at[at], in_sem.at[side, h])
+
+    inputs = ((IMAGE, pic, image_raw), (TEXT, cap, text_raw))
+    for h in range(2):
+        for which in inputs:
+            load(h, *which).start()
 
     barrier = pltpu.get_barrier_semaphore()
     others = [who["ahead"], who["behind"], who["after"], who["before"]] + who["along"][1:]
@@ -88,25 +99,33 @@
             device_id_type=MESH,
         )
 
-    for side, raw in ((IMAGE, image_raw), (TEXT, text_raw)):
-        loads[side].wait()
-
-        @pl.loop(0, 2)
-        def _(k):
-            at = pl.ds(k * half, half)
+    def normalize(h):
+        at = pl.ds(h * half, half)
+        for side, src, raw in inputs:
+            load(h, side, src, raw).wait()
             rawf = raw[at].astype(jnp.float32)
             scale = 1.0 / jnp.sqrt(jnp.sum(rawf * rawf, axis=-1, keepdims=True) + 1e-06)
             unit[side, at] = (rawf * scale).astype(jnp.bfloat16)
 
+    normalize(0)
     pl.semaphore_wait(barrier, len(others))
-
-    for k in range(WINDOW):
-        for side in (IMAGE, TEXT):
-            z_copy(side, k).start()
+    for h in range(2):
+        if h == 1:
+            normalize(1)
+        for k in range(h * CHUNKS // 2, (h + 1) * CHUNKS // 2):
+            for side in (IMAGE, TEXT):
+
+                @pl.when(k < who["window"])
+                def _():
+                    z_copy(side, k).start()
+
+                @pl.when(k < who["lead"][side])
+                def _():
+                    g_copy(side, k).start()
 
     @pl.loop(0, CHUNKS)
     def _(k):
-        for d in range(1, NX):
+        for d in X_ORDER:
 
             @pl.when(x + d < NX)
             def _():
@@ -161,40 +180,29 @@
             for d in range(1, NX):
                 x_copy(side, d, k, False).wait_recv()
 
-    def start_near(k):
-        for side in (IMAGE, TEXT):
-            g_copy(side, k).start()
-
     @pl.loop(0, CHUNKS)
     def _(k):
         for side in (IMAGE, TEXT):
             z_copy(side, k).wait_recv()
-        for d in range(1, NX):
-
-            @pl.when(x + d >= NX)
+            for d in X_ORDER:
+
+                @pl.when(x + d >= NX if side == TEXT else x + d < NX)
+                def _():
+                    x_copy(side, d, k, True).start()
+
+            @pl.when(k + who["window"] < CHUNKS)
             def _():
-                x_copy(TEXT, d, k, True).start()
-
-            @pl.when(x + d < NX)
+                z_copy(side, k + who["window"]).start()
+
+            @pl.when(k + who["lead"][side] < CHUNKS)
             def _():
-                x_copy(IMAGE, d, k, True).start()
-
-        @pl.when(k + WINDOW < CHUNKS)
-        def _():
-            for side in (IMAGE, TEXT):
-                z_copy(side, k + WINDOW).start()
-
-        @pl.when(k >= G_LAG)
-        def _():
-            start_near(k - G_LAG)
+                g_copy(side, k + who["lead"][side]).start()
 
         @pl.when(k > 0)
         def _():
             await_round(k - 1)
             score(pl.ds((k - 1) * per, per))
 
-    for k in range(CHUNKS - G_LAG, CHUNKS):
-        start_near(k)
     for k in range(CHUNKS // 2):
         for side in (TEXT, IMAGE):
             g_copy(side, k).wait_recv()
@@ -250,7 +258,7 @@
     vmem, any_ = pl.BlockSpec(memory_space=pltpu.VMEM), pl.BlockSpec(memory_space=pl.ANY)
     hbm = pl.BlockSpec(memory_space=pltpu.HBM)
     dma = pltpu.SemaphoreType.DMA
-    scalars = jnp.stack([sharpness_factor, additive_shift_term]).astype(jnp.float32)
+    smem = pl.BlockSpec(memory_space=pltpu.SMEM)
     sums = pl.pallas_call(
         exchange,
         out_shape=(
@@ -260,13 +268,13 @@
             pltpu.VMEM((rows, width), kind),
             pltpu.VMEM((1, rows), jnp.float32),
         ),
-        in_specs=[pl.BlockSpec(memory_space=pltpu.SMEM), hbm, hbm],
+        in_specs=[smem, smem, hbm, hbm],
         out_specs=(vmem,) * 5,
         scratch_shapes=[
             pltpu.VMEM((2, rows, width), jnp.bfloat16),
             pltpu.VMEM((2, (NX + 1) * rows, width), jnp.bfloat16),
             pltpu.VMEM((rows, min(128, NX * part)), jnp.float32),
-            dma((2,)),
+            dma((2, 2)),
             dma((2, CHUNKS)),
             dma((2, CHUNKS)),
             dma((2, NX - 1, CHUNKS)),
@@ -279,7 +287,8 @@
         ),
         name="exchange",
     )(
-        scalars,
+        sharpness_factor.reshape(1, 1),
+        additive_shift_term.reshape(1, 1),
         pltpu.with_memory_space_constraint(picture_embeds_raw, pltpu.HBM),
         pltpu.with_memory_space_constraint(caption_embeds_raw, pltpu.HBM),
     )

time: 90.9 us -> 88.5 us (0.974)
  the two profiles are of different devices: /device:TPU:8 before, /device:TPU:241 now
where the time goes in v3:
time: 88.5 us; the launch traced here: 88.3 us
  Pallas kernels  86.4 us (98%)
  between operations  1.93 us (2%)
    pallas_call x1, Pallas kernels, on_device(): pl.pallas_call(exchange, out_shape=(pltpu.VMEM((rows, width), jnp.float32...  84.3 us
    pallas_call x1, Pallas kernels, on_device(): pl.pallas_call(finish, out_shape=(jax.ShapeDtypeStruct((rows,), jnp.float...  2.13 us

profile of v3, /device:TPU:241, one launch (start us, length us, event | category | flops | bytes accessed | tf_op | source)
XLA Modules:
  0.0 88.3 jit_solution(3382638791259589040)
XLA Ops:
  1.9 84.3 %exchange.1 = (f32[256,1152]{1,0:T(8,128)S(1)}, f32[256,1152]{1,0:T(8,128)S(1)}, bf16[256,1152]{1,0:T(8,128)(2,1)S(1)}, bf16[256,1152]{1,0:T(8,128)(2,1)S(1)}, f32[1,256]{1,0:T(1,128)S(1)}) custom-call(f32[1,1]{1,0:T(1,128)} %bitcast.2.sharp_ref, f32[1,1]{1,0:T(1,128)} %bitcast.3.shift_ref, bf16[256,1152]{1,0:T(8,128)(2,1)} %pic.1, bf16[256,1152]{1,0:T(8,128)(2,1)} %cap.1), custom_call_target="tpu_custom_call" | custom-call | tf_op jit(solution)/shard_map/exchange/pallas_call | solution.py:262
  86.2 2.1 %finish.1 = (f32[256]{0:T(256)}, bf16[256,1152]{1,0:T(8,128)(2,1)}, bf16[256,1152]{1,0:T(8,128)(2,1)}) custom-call(f32[256,1152]{1,0:T(8,128)S(1)} %get-tuple-element.8.image_acc, f32[256,1152]{1,0:T(8,128)S(1)} %get-tuple-element.9.text_acc, bf16[256,1152]{1,0:T(8,128)(2,1)S(1)} %get-tuple-element.10.image_raw, ...), custom_call_target="tpu_custom_call" | custom-call | tf_op jit(solution)/shard_map/finish/pallas_call | solution.py:295

commit v4 on v3

--- a/solution.py
+++ b/solution.py
@@ -53,12 +53,17 @@
     who = partners()
     x = who["x"]
 
+    pieces = ((0, 1), (1, CHUNKS // 2), (CHUNKS // 2, CHUNKS))
+
+    def rows_of(h):
+        return pl.ds(pieces[h][0] * part, (pieces[h][1] - pieces[h][0]) * part)
+
     def load(h, side, src, dst):
-        at = pl.ds(h * half, half)
+        at = rows_of(h)
         return pltpu.make_async_copy(src.at[at], dst.at[at], in_sem.at[side, h])
 
     inputs = ((IMAGE, pic, image_raw), (TEXT, cap, text_raw))
-    for h in range(2):
+    for h in range(len(pieces)):
         for which in inputs:
             load(h, *which).start()
 
@@ -100,7 +105,7 @@
         )
 
     def normalize(h):
-        at = pl.ds(h * half, half)
+        at = rows_of(h)
         for side, src, raw in inputs:
             load(h, side, src, raw).wait()
             rawf = raw[at].astype(jnp.float32)
@@ -109,10 +114,10 @@
 
     normalize(0)
     pl.semaphore_wait(barrier, len(others))
-    for h in range(2):
-        if h == 1:
-            normalize(1)
-        for k in range(h * CHUNKS // 2, (h + 1) * CHUNKS // 2):
+    for h, piece in enumerate(pieces):
+        if h > 0:
+            normalize(h)
+        for k in range(*piece):
             for side in (IMAGE, TEXT):
 
                 @pl.when(k < who["window"])
@@ -175,6 +180,13 @@
             (back * sharp).astype(jnp.bfloat16), images, preferred_element_type=jnp.float32
         )
 
+    def await_sent(k):
+        for side in (IMAGE, TEXT):
+            z_copy(side, k).wait_send()
+            g_copy(side, k).wait_send()
+            for d in range(1, NX):
+                x_copy(side, d, k, False).wait_send()
+
     def await_round(k):
         for side in (TEXT, IMAGE):
             for d in range(1, NX):
@@ -202,6 +214,10 @@
         def _():
             await_round(k - 1)
             score(pl.ds((k - 1) * per, per))
+
+    @pl.loop(0, CHUNKS - 2)
+    def _(k):
+        await_sent(k)
 
     for k in range(CHUNKS // 2):
         for side in (TEXT, IMAGE):
@@ -215,13 +231,8 @@
 
     loss_out[...] = jnp.sum(loss_acc[...].T, axis=0, keepdims=True)
 
-    @pl.loop(0, CHUNKS)
-    def _(k):
-        for side in (IMAGE, TEXT):
-            z_copy(side, k).wait_send()
-            g_copy(side, k).wait_send()
-            for d in range(1, NX):
-                x_copy(side, d, k, False).wait_send()
+    for k in range(CHUNKS - 2, CHUNKS):
+        await_sent(k)
 
 
 def finish(
@@ -274,7 +285,7 @@
             pltpu.VMEM((2, rows, width), jnp.bfloat16),
             pltpu.VMEM((2, (NX + 1) * rows, width), jnp.bfloat16),
             pltpu.VMEM((rows, min(128, NX * part)), jnp.float32),
-            dma((2, 2)),
+            dma((2, 3)),
             dma((2, CHUNKS)),
             dma((2, CHUNKS)),
             dma((2, NX - 1, CHUNKS)),

time: 88.5 us -> 88.5 us (level)
  no operation moved by 1% of the time
where the time goes in v4:
time: 88.5 us; the launch traced here: 88.3 us
  Pallas kernels  86.4 us (98%)
  between operations  1.93 us (2%)
    pallas_call x1, Pallas kernels, on_device(): pl.pallas_call(exchange, out_shape=(pltpu.VMEM((rows, width), jnp.float32...  84.3 us
    pallas_call x1, Pallas kernels, on_device(): pl.pallas_call(finish, out_shape=(jax.ShapeDtypeStruct((rows,), jnp.float...  2.13 us

profile of v4, /device:TPU:241, one launch (start us, length us, event | category | flops | bytes accessed | tf_op | source)
XLA Modules:
  0.0 88.3 jit_solution(5755546408513932083)
XLA Ops:
  1.9 84.3 %exchange.1 = (f32[256,1152]{1,0:T(8,128)S(1)}, f32[256,1152]{1,0:T(8,128)S(1)}, bf16[256,1152]{1,0:T(8,128)(2,1)S(1)}, bf16[256,1152]{1,0:T(8,128)(2,1)S(1)}, f32[1,256]{1,0:T(1,128)S(1)}) custom-call(f32[1,1]{1,0:T(1,128)} %bitcast.2.sharp_ref, f32[1,1]{1,0:T(1,128)} %bitcast.3.shift_ref, bf16[256,1152]{1,0:T(8,128)(2,1)} %pic.1, bf16[256,1152]{1,0:T(8,128)(2,1)} %cap.1), custom_call_target="tpu_custom_call" | custom-call | tf_op jit(solution)/shard_map/exchange/pallas_call | solution.py:273
  86.2 2.1 %finish.1 = (f32[256]{0:T(256)}, bf16[256,1152]{1,0:T(8,128)(2,1)}, bf16[256,1152]{1,0:T(8,128)(2,1)}) custom-call(f32[256,1152]{1,0:T(8,128)S(1)} %get-tuple-element.8.image_acc, f32[256,1152]{1,0:T(8,128)S(1)} %get-tuple-element.9.text_acc, bf16[256,1152]{1,0:T(8,128)(2,1)S(1)} %get-tuple-element.10.image_raw, ...), custom_call_target="tpu_custom_call" | custom-call | tf_op jit(solution)/shard_map/finish/pallas_call | solution.py:306
